TPU v7x, 32 devices: a whole 2x2x4 slice. The times are simulated.
32 devices in a mesh: groups: 2 (over x), bond: 8 (over z, y), term: 2 (over core).
Axes of the slice: x: 2, y: 2, z: 4, core: 2. Of those that a mesh axis runs over, the one named last changes fastest.
Arguments:
- psi_blocks: float32 [768, 128, 128], P(('groups', 'bond')), parts along dimension 0, may hold values from -6 to 6
- left_env: float32 [12, 48, 128, 128], P('term', ('groups', 'bond')), parts along dimension 1, may hold values from -0.0140625 to 4
- right_env: float32 [12, 48, 128, 128], P('term', ('groups', 'bond')), parts along dimension 1, may hold values from -0.001171875 to 0.33333333
- owner_route: int32 [768, 1], P(('groups', 'bond')), parts along dimension 0, may hold values from 0 to 7; in each aligned block of 48 rows (0 to 47, 48 to 95, ...) at most 9 rows name the same one
- local_sector: int32 [768], P(('groups', 'bond')), parts along dimension 0, may hold values from 0 to 2
Outputs:
- residual: float32 [768, 128, 128], P(('groups', 'bond')), parts along dimension 0
- theta: float32 [2], P('groups'), parts along dimension 0
There are 2 independent parts, one for each index of `groups`. A program takes and returns all parts, laid end to end along the dimension named above; each array names one. Nothing has to cross between parts.
Inputs may be any that keep to these rules, and one draw needn't show every extreme that they name: `owner_route`: among the 48 blocks of one device, no owner index is named more than 9 times, a bound that some block reaches.
All inputs are finite; a program needn't handle non-finite values.
Results may differ from a plain program's by a relative error of at most 0.0003.
Values sent between devices are 32-bit elements; how exact they have to be, the bound alone decides.
A program may use at most 256 MiB of HBM per device.

v0:
```python
import jax
import jax.numpy as jnp
from jax import lax
from jax.sharding import PartitionSpec as P


def body(psi_blocks, left_env, right_env, owner_route, local_sector):
    block_count, states, _ = psi_blocks.shape
    term_count, sector_count = (left_env.shape[0], left_env.shape[1])
    physical = block_count // sector_count
    bond_count = lax.axis_size("bond")
    capacity = max(2, 3 * block_count // (2 * bond_count))
    grouped = psi_blocks.reshape(sector_count, physical, states, states)
    products = jnp.einsum("asij,spjk->spaik", left_env, grouped, precision=lax.Precision.HIGHEST)
    products = products.reshape(block_count, term_count, states, states)
    owner = owner_route[:, 0]
    onehot = (owner[:, None] == jnp.arange(bond_count, dtype=jnp.int32)[None, :]).astype(jnp.int32)
    rank = jnp.sum(jnp.cumsum(onehot, axis=0) * onehot, axis=1) - 1
    slot = owner * capacity + rank
    outgoing = (
        jnp.zeros((bond_count * capacity, term_count, states, states), jnp.float32)
        .at[slot]
        .set(products)
    )
    sector_ids = jnp.zeros((bond_count * capacity,), jnp.int32).at[slot].set(local_sector)
    outgoing = outgoing.reshape(bond_count, capacity, term_count, states, states)
    sector_ids = sector_ids.reshape(bond_count, capacity)
    chosen = jnp.take(
        right_env,
        lax.all_to_all(sector_ids, "bond", split_axis=0, concat_axis=0, tiled=True),
        axis=1,
    )
    chosen = jnp.transpose(chosen, (1, 2, 0, 3, 4))
    fetched = lax.all_to_all(chosen, "bond", split_axis=0, concat_axis=0, tiled=True)
    back = jnp.einsum("ncaij,ncajk->ncik", outgoing, fetched, precision=lax.Precision.HIGHEST)
    partial_blocks = back.reshape(bond_count * capacity, states, states)[slot]
    hpsi = lax.psum(partial_blocks, "term")
    sums = lax.psum((jnp.sum(psi_blocks * hpsi), jnp.sum(psi_blocks * psi_blocks)), "bond")
    theta = sums[0] / sums[1]
    residual = hpsi - theta * psi_blocks
    return (residual, jnp.reshape(theta, (1,)))


def solution(mesh):
    return jax.shard_map(
        body,
        mesh=mesh,
        in_specs=(
            P(("groups", "bond"), None, None),
            P("term", ("groups", "bond"), None, None),
            P("term", ("groups", "bond"), None, None),
            P(("groups", "bond"), None),
            P(("groups", "bond")),
        ),
        out_specs=(P(("groups", "bond"), None, None), P("groups")),
        check_vma=False,
    )
```

profile of v0, /device:TPU:0, one launch (start us, length us, event | category | flops | bytes accessed | tf_op | source)
XLA Modules:
  0.0 774.7 jit_solution(14993438905080370169)
XLA Ops:
  7.2 0.8 fusion.2
  8.0 0.1 reduce_window_sum.11
  8.1 0.8 select_reduce_fusion
  8.9 0.7 fusion.3
  9.6 0.9 scatter_custom_fusion.1
  10.4 0.1 all_to_all.13
  10.5 13.5 %all_to_all.20 = s32[8,1,9]{2,1,0:T(1,128)S(1)} all-to-all(s32[8,1,9]{2,1,0:T(1,128)S(1)} %bitcast.41), channel_id=1, replica_groups=mesh['groups'=2,'bond'=8,'term'=2] {'bond'}, dimensions={0} | all-to-all | bytes 576 | tf_op jit(solution)/shard_map/all_to_all | solution.py:30
  24.1 0.1 reshape.73
  24.2 13.0 %gather_fusion = f32[72,6,128,128]{3,2,1,0:T(8,128)} fusion(f32[6,3,128,128]{3,2,1,0:T(8,128)S(1)} %copy-done, s32[1024]{0:T(1024)S(1)} %pad_clamp_fusion.1), kind=kCustom, calls=%fused_computation | custom fusion | bytes 56623392 | tf_op jit(solution)/shard_map/jit(_take)/gather | solution.py:28
  37.2 20.8 %broadcast_select_fusion = f32[8,9,6,128,128]{4,3,2,1,0:T(8,128)} fusion(f32[8,9,6,128,128]{4,3,2,1,0:T(8,128)} %bitcast.35, pred[8,9]{1,0:T(8,128)(4,1)S(1)} %compare_and_fusion), kind=kLoop, calls=%fused_computation.4 | loop fusion | flops 7077888 | bytes 56623176 | tf_op jit(solution)/shard_map/jit(_take)/select_n | solution.py:28
  58.1 6.8 all-to-all-start.1
  64.9 0.2 all-reduce.3.cloned.1.call-start
  65.1 19.1 %fusion = f32[3,16,128,6,128]{4,2,3,1,0:T(8,128)} fusion(f32[3,16,128,128,1]{3,2,4,1,0:T(8,128)} %bitcast.37, f32[6,3,128,128]{3,2,1,0:T(8,128)S(1)} %copy-done.2), kind=kOutput, calls=%fused_computation.8 | convolution fusion | flops 7247757312 | bytes 23199744 | tf_op jit(solution)/shard_map/asij,spjk->spaik/dot_general | solution.py:14
  84.3 18.6 %copy.14 = f32[48,6,128,128]{3,2,1,0:T(8,128)} copy(f32[48,6,128,128]{2,3,1,0:T(8,128)} %bitcast.36) | data formatting | bytes 37748736 | tf_op jit(solution)/shard_map/reshape | solution.py:15
  102.9 13.0 %broadcast_in_dim.20 = f32[72,6,128,128]{3,2,1,0:T(8,128)} broadcast(f32[]{:T(128)} %constant.11.clone.1), dimensions={} | broadcast | bytes 28311556 | tf_op jit(solution)/shard_map/broadcast_in_dim | solution.py:21
  115.8 38.6 %scatter_fusion = f32[72,6,128,128]{3,2,1,0:T(8,128)} fusion(f32[72,6,128,128]{3,2,1,0:T(8,128)} %broadcast_in_dim.20, s32[48]{0:T(128)S(1)} %fusion.3, f32[48,6,128,128]{3,2,1,0:T(8,128)} %copy.14), kind=kCustom, calls=%fused_computation.2 | custom fusion | bytes 56623296 | tf_op jit(solution)/shard_map/scatter | solution.py:23
  154.4 519.3 %all-to-all-done.1 = f32[8,9,6,128,128]{4,3,2,1,0:T(8,128)} async-done(((f32[8,9,6,128,128]{4,3,2,1,0:T(8,128)}), f32[8,9,6,128,128]{4,3,2,1,0:T(8,128)}, u32[]{:S(2)}, u32[]{:S(2)}) %all-to-all-start.1) | async-done | bytes 28311584 | tf_op jit(solution)/shard_map/all_to_all | solution.py:34
  673.7 32.8 %fusion.6 = f32[8,9,128,128,1]{3,2,4,1,0:T(8,128)} fusion(f32[8,9,6,128,128]{4,3,2,1,0:T(8,128)} %bitcast.34, f32[8,9,6,128,128]{4,3,2,1,0:T(8,128)} %all-to-all-done.1), kind=kOutput, calls=%fused_computation.23 | convolution fusion | flops 10871635968 | bytes 61341696 | tf_op jit(solution)/shard_map/ncaij,ncajk->ncik/dot_general | solution.py:35
  706.5 4.7 gather_fusion.1
  711.3 0.0 all-reduce.3.cloned.1.call-update
  711.3 22.2 %all-reduce.3.cloned.1.call-done = f32[48,128,128]{2,1,0:T(8,128)} async-done(((f32[48,128,128]{2,1,0:T(8,128)}), f32[48,128,128]{2,1,0:T(8,128)}) %all-reduce.3.cloned.1.call-update) | async-done | bytes 3145744 | tf_op jit(solution)/shard_map/psum | solution.py:37
  733.5 4.3 multiply_reduce_fusion
  737.7 22.2 %all-reduce = (f32[]{:T(128)}, f32[]{:T(128)}) all-reduce(f32[]{:T(128)} %get-tuple-element.3, f32[]{:T(128)} %get-tuple-element.2), channel_id=1, replica_groups=mesh['groups'=2,'bond'=8,'term'=2] {'bond'}, use_global_device_ids=true, to_apply=%region_6.7 | all-reduce | flops 2 | bytes 16 | tf_op jit(solution)/shard_map/psum | solution.py:38
  761.4 5.3 multiply_subtract_fusion
  (10 shorter events, 0.0 us)
Async XLA Ops:
  7.2 17.0 %copy-start = (f32[6,3,128,128]{3,2,1,0:T(8,128)S(1)}, f32[6,3,128,128]{3,2,1,0:T(8,128)}, u32[]{:S(2)}) copy-start(f32[6,3,128,128]{3,2,1,0:T(8,128)} %param.7) | copy-start | bytes 3538948
  58.1 7.0 copy-start.2
  58.1 615.7 %all-to-all-start.1 = ((f32[8,9,6,128,128]{4,3,2,1,0:T(8,128)}), f32[8,9,6,128,128]{4,3,2,1,0:T(8,128)}, u32[]{:S(2)}, u32[]{:S(2)}) async-start(f32[8,9,6,128,128]{4,3,2,1,0:T(8,128)} %broadcast_select_fusion), calls=%async_computation.1 | async-start | bytes 56623104 | tf_op jit(solution)/shard_map/all_to_all | solution.py:34
  64.9 668.6 %all-reduce.3.cloned.1.call-start = ((), (), s32[]{:S(2)}) async-start(), calls=%async_computation.2 | async-start | bytes 6291456 | tf_op jit(solution)/shard_map/psum | solution.py:37
  760.0 6.8 copy-start.1
Sparse Core Ops, SparseCore 0:
  711.4 21.9 all-reduce.2
where the time goes:
time: 776 us; the launch traced here: 775 us
  waiting for transfers between devices  541 us (70%)
  local copies, waits for them, and re-layouts  89 us (11%)
  matrix products  51.9 us (7%)
  blocking collectives  35.8 us (5%)
  other arithmetic  32.9 us (4%)
  between operations  16.6 us (2%)
    all_to_all x1, waiting for transfers between devices, body(): lax.all_to_all(chosen, 'bond', split_axis=0, concat_axis=0, tiled=True)  519 us
    scatter x1, local copies, waits for them, and re-layouts, body(): outgoing = jnp.zeros((bond_count * capacity, term_count, states, states),...  38.6 us
    dot_general x1, matrix products, body(): jnp.einsum('ncaij,ncajk->ncik', outgoing, fetched, precision=lax.Precisio...  32.8 us
    psum x1, blocking collectives, body(): lax.psum((jnp.sum(psi_blocks * hpsi), jnp.sum(psi_blocks * psi_blocks)),...  22.2 us
    psum x1, waiting for transfers between devices, body(): hpsi = lax.psum(partial_blocks, 'term')  22.2 us
    select_n x2, other arithmetic, body(): jnp.take(right_env, lax.all_to_all(sector_ids, 'bond', split_axis=0, conc...  20.9 us
    dot_general x1, matrix products, body(): jnp.einsum('asij,spjk->spaik', left_env, grouped, precision=lax.Precision...  19.1 us
    reshape x1, local copies, waits for them, and re-layouts, body(): products = products.reshape(block_count, term_count, states, states)  18.6 us
  transfers between devices with their start and end apart: 2, of which 2 were waited for; matrix products, arithmetic and copies ran while one was open for 12% of the time, Pallas kernels for 0%

commit v1 on v0

v1 whole, which is shorter than its diff:
```python
import functools

import jax
import jax.numpy as jnp
from jax import lax
from jax.experimental import pallas as pl
from jax.experimental.pallas import tpu as pltpu
from jax.sharding import PartitionSpec as P

MESH = pl.DeviceIdType.MESH
UP, DOWN, ACROSS = 0, 1, 2
NZ, NY = 4, 2
AHEAD = 2
F32, BF16 = jnp.float32, jnp.bfloat16


def split(x):
    hi = x.astype(BF16)
    lo = (x - hi.astype(F32)).astype(BF16)
    return hi, lo


def pair_rhs(x):
    hi, lo = split(x)
    row = jnp.concatenate([hi, lo], axis=1)
    return jnp.concatenate([row, row], axis=0)


def fold(o):
    n = o.shape[1] // 2
    return o[:, :n] + o[:, n:]


def rows_sum(x):
    r, c = x.shape
    return jnp.sum(x.reshape(r // 8, 8, c), axis=0)


def kernel(terms, sectors, phys, idx_ref, psi_hbm, left_hbm, right_hbm,
           part_hbm, other_hbm, theta_ref, *scratch):
    gathered = scratch[:terms]
    (psi_v, left_v, lefts, prods, acc, dots,
     recv, send, psi_sem, left_sem, own_sem, xsend, xrecv, out_sem, dsend, drecv) = scratch[terms:]
    bond_count = NZ * NY
    blocks = sectors * phys
    states = psi_v.shape[1]
    me = lax.axis_index("bond")
    core = lax.axis_index("term")
    z, y = me // NY, me % NY
    last = terms - 1

    def rows(src):
        return pl.ds(src * sectors, sectors)

    left_copy = pltpu.make_async_copy(left_hbm, left_v, left_sem)
    left_copy.start()
    psi_copies = []
    for s in range(sectors):
        c = pltpu.make_async_copy(psi_hbm.at[pl.ds(s * phys, phys)], psi_v.at[pl.ds(s * phys, phys)], psi_sem.at[s])
        c.start()
        psi_copies.append(c)
    own_copies = []
    for a in range(terms):
        c = pltpu.make_async_copy(right_hbm.at[a], gathered[a].at[rows(me)], own_sem.at[a])
        c.start()
        own_copies.append(c)

    barrier = pltpu.get_barrier_semaphore()
    peers = []
    for k in range(1, 2 * bond_count):
        flat = lax.rem(me * 2 + core + k, 2 * bond_count)
        peers.append((flat // 2, flat % 2))
    for pb, pt in peers:
        pl.semaphore_signal(barrier, inc=1, device_id={"bond": pb, "term": pt}, device_id_type=MESH)
    pl.semaphore_wait(barrier, len(peers))

    def chunk(a, src, way, own=False):
        if way == UP:
            to = me + NY
        elif way == DOWN:
            to = me - NY
        else:
            to = z * NY + (1 - y)
        here = right_hbm.at[a] if own else gathered[a].at[rows(src)]
        return pltpu.make_async_remote_copy(
            src_ref=here, dst_ref=gathered[a].at[rows(src)],
            send_sem=send.at[a, src, way], recv_sem=recv.at[a, src],
            device_id={"bond": to}, device_id_type=MESH)

    sent = []

    def go(cond, a, src, way, own=False):
        def start():
            chunk(a, src, way, own).start()

        if cond is None:
            start()
        else:
            pl.when(cond)(start)
        sent.append((cond, a, src, way, own))

    def arrived(a, src):
        chunk(a, src, ACROSS).wait_recv()

    partner = z * NY + (1 - y)

    def send_own(a):
        if a < last:
            go(z < NZ - 1, a, me, UP, True)
            go(z > 0, a, me, DOWN, True)
            go(None, a, me, ACROSS, True)
        else:
            go(z < NZ - 1, a, me, UP, True)
            go(z > 0, a, me, DOWN, True)
            arrived(a, partner)
            go(z < NZ - 1, a, partner, UP)
            go(z > 0, a, partner, DOWN)

    def prepare_left():
        left_copy.wait()
        for s in range(sectors):
            for a in range(terms):
                hi, lo = split(left_v[a, s])
                lefts[s, a * states:(a + 1) * states, :] = jnp.concatenate([hi, lo], axis=1)

    def left_piece(s, lo, count):
        def body(i, norm):
            b = s * phys + lo + i
            x = psi_v[b]
            t = fold(jnp.dot(lefts[s], pair_rhs(x), preferred_element_type=F32))
            hi, low = split(t)
            both = jnp.concatenate([hi, low], axis=1)
            for a in range(terms):
                prods[a, b] = both[a * states:(a + 1) * states]
            return norm + rows_sum(x * x)

        norm = lax.fori_loop(0, count, body, jnp.zeros((8, states), F32))
        dots[me * 2 + core, 8:16, :] += norm

    def right_piece(a, first, count):
        def body(i, dot):
            b = first + i
            w = pair_rhs(gathered[a][idx_ref[b]])
            v = fold(jnp.dot(prods[a, b], w, preferred_element_type=F32))
            if a > 0:
                v = v + acc[b]
            acc[b] = v
            if a == last:
                dot = dot + rows_sum(v * psi_v[b])
            return dot

        dot = lax.fori_loop(0, count, body, jnp.zeros((8, states), F32))
        if a == last:
            dots[me * 2 + core, 0:8, :] += dot

    def across_done(a):
        own_copies[a].wait()
        for zz in range(NZ):
            arrived(a, zz * NY + (1 - y))

    exchange = []

    def exchange_piece(k, first, count):
        c = pltpu.make_async_remote_copy(
            src_ref=acc.at[pl.ds(first, count)], dst_ref=other_hbm.at[pl.ds(first, count)],
            send_sem=xsend.at[k], recv_sem=xrecv.at[k],
            device_id={"term": 1 - core}, device_id_type=MESH)
        c.start()
        d = pltpu.make_async_copy(acc.at[pl.ds(first, count)], part_hbm.at[pl.ds(first, count)], out_sem.at[k])
        d.start()
        exchange.append((c, d))

    half = phys // 4
    left_work = []
    for s in range(sectors):
        for q in range(4):
            def piece(s=s, q=q):
                if q == 0:
                    psi_copies[s].wait()
                left_piece(s, q * half, half)
            left_work.append(piece)
    eighth = blocks // 6

    def right_work(a):
        out = []
        for q in range(6):
            def piece(a=a, q=q):
                if q == 0:
                    across_done(a)
                right_piece(a, q * eighth, eighth)
            out.append(piece)
        return out

    slots = {(a, k): [] for a in range(terms) for k in range(6)}
    for i, w in enumerate(left_work):
        slots[(i // 6, i % 6)].append(w)
    for a in range(terms - 2):
        for i, w in enumerate(right_work(a)):
            slots[(a + 2, i)].append(w)

    go(None, 0, me, ACROSS, True)
    go(z < NZ - 1, 0, me, UP, True)
    go(z > 0, 0, me, DOWN, True)
    go(None, last, me, ACROSS, True)
    for a in range(1, AHEAD):
        send_own(a)
    dots[me * 2 + core] = jnp.zeros((16, states), F32)
    prepare_left()

    for a in range(terms):
        if a + AHEAD < terms:
            send_own(a + AHEAD)
        for h in range(1, NZ):
            ys = [y] if a < last else [y, 1 - y]
            below, above = z >= h, z + h < NZ

            @pl.when(below)
            def _():
                for yy in ys:
                    arrived(a, (z - h) * NY + yy)

            for yy in ys:
                go(below & (z < NZ - 1), a, (z - h) * NY + yy, UP)
            if a < last:
                go(below, a, (z - h) * NY + y, ACROSS)
            for w in slots[(a, 2 * h - 2)]:
                w()

            @pl.when(above)
            def _():
                for yy in ys:
                    arrived(a, (z + h) * NY + yy)

            for yy in ys:
                go(above & (z > 0), a, (z + h) * NY + yy, DOWN)
            if a < last:
                go(above, a, (z + h) * NY + y, ACROSS)
            for w in slots[(a, 2 * h - 1)]:
                w()

    for w in right_work(last - 1):
        w()
    own_copies[last].wait()
    for q in range(6):
        right_piece(last, q * eighth, eighth)
        exchange_piece(q, q * eighth, eighth)

    mine = me * 2 + core
    dot_copies = []
    for k, (pb, pt) in enumerate(peers):
        c = pltpu.make_async_remote_copy(
            src_ref=dots.at[mine], dst_ref=dots.at[mine],
            send_sem=dsend.at[k], recv_sem=drecv.at[mine],
            device_id={"bond": pb, "term": pt}, device_id_type=MESH)
        c.start()
        dot_copies.append(c)
    for k, (pb, pt) in enumerate(peers):
        theirs = pb * 2 + pt
        pltpu.make_async_remote_copy(
            src_ref=dots.at[theirs], dst_ref=dots.at[theirs],
            send_sem=dsend.at[k], recv_sem=drecv.at[theirs],
            device_id={"bond": pb, "term": pt}, device_id_type=MESH).wait_recv()
    total = dots[0]
    for i in range(1, 2 * bond_count):
        total = total + dots[i]
    dot = jnp.sum(total[0:8], axis=(0, 1), keepdims=True)
    norm = jnp.sum(total[8:16], axis=(0, 1), keepdims=True) * 0.5
    theta_ref[...] = jnp.broadcast_to(dot / norm, theta_ref.shape)

    for cond, a, src, way, own in sent:
        def finish(a=a, src=src, way=way, own=own):
            chunk(a, src, way, own).wait_send()

        if cond is None:
            finish()
        else:
            pl.when(cond)(finish)
    for c, d in exchange:
        c.wait()
        d.wait()
    for c in dot_copies:
        c.wait_send()


def fast_body(psi_blocks, left_env, right_env, owner_route, local_sector):
    blocks, states, _ = psi_blocks.shape
    terms, sectors = left_env.shape[0], left_env.shape[1]
    phys = blocks // sectors
    bond_count = NZ * NY
    right_sector = owner_route[:, 0] * sectors + local_sector
    any_spec = pl.BlockSpec(memory_space=pl.ANY)
    block_shape = jax.ShapeDtypeStruct((blocks, states, states), F32)
    dma = pltpu.SemaphoreType.DMA
    part, other, theta = pl.pallas_call(
        functools.partial(kernel, terms, sectors, phys),
        out_shape=(block_shape, block_shape, jax.ShapeDtypeStruct((8, 128), F32)),
        in_specs=[pl.BlockSpec(memory_space=pltpu.SMEM), any_spec, any_spec, any_spec],
        out_specs=(any_spec, any_spec, pl.BlockSpec(memory_space=pltpu.VMEM)),
        scratch_shapes=[pltpu.VMEM((bond_count * sectors, states, states), F32) for _ in range(terms)] + [
            pltpu.VMEM((blocks, states, states), F32),
            pltpu.VMEM((terms, sectors, states, states), F32),
            pltpu.VMEM((sectors, terms * states, 2 * states), BF16),
            pltpu.VMEM((terms, blocks, states, 2 * states), BF16),
            pltpu.VMEM((blocks, states, states), F32),
            pltpu.VMEM((2 * bond_count, 16, states), F32),
            dma((terms, bond_count)),
            dma((terms, bond_count, 3)),
            dma((sectors,)),
            dma,
            dma((terms,)),
            dma((6,)),
            dma((6,)),
            dma((6,)),
            dma((2 * bond_count - 1,)),
            dma((2 * bond_count,)),
        ],
        compiler_params=pltpu.CompilerParams(
            collective_id=0, has_side_effects=True, vmem_limit_bytes=56 * 1024 * 1024),
        cost_estimate=pl.CostEstimate(
            flops=4 * terms * blocks * states ** 3, bytes_accessed=20_000_000, transcendentals=0),
    )(right_sector, psi_blocks, left_env, right_env)
    value = theta[0, 0]
    residual = part + other - value * psi_blocks
    return residual, jnp.reshape(value, (1,))


def general_body(psi_blocks, left_env, right_env, owner_route, local_sector):
    blocks, states, _ = psi_blocks.shape
    sectors = left_env.shape[1]
    phys = blocks // sectors
    right_sector = owner_route[:, 0] * sectors + local_sector
    rights = lax.all_gather(right_env, "bond", axis=1, tiled=True)
    lefts = jnp.arange(blocks, dtype=jnp.int32) // phys

    def one(items):
        block, li, ri = items
        inner = jnp.einsum("aij,jk->aik", jnp.take(left_env, li, axis=1), block, precision=lax.Precision.HIGHEST)
        return jnp.einsum("aik,akl->il", inner, jnp.take(rights, ri, axis=1), precision=lax.Precision.HIGHEST)

    hpsi = lax.psum(lax.map(one, (psi_blocks, lefts, right_sector)), "term")
    sums = lax.psum((jnp.sum(psi_blocks * hpsi), jnp.sum(psi_blocks * psi_blocks)), "bond")
    theta = sums[0] / sums[1]
    return hpsi - theta * psi_blocks, jnp.reshape(theta, (1,))


def solution(mesh):
    fits = mesh.shape["bond"] == NZ * NY and mesh.shape["term"] == 2
    return jax.shard_map(
        fast_body if fits else general_body,
        mesh=mesh,
        in_specs=(
            P(("groups", "bond"), None, None),
            P("term", ("groups", "bond"), None, None),
            P("term", ("groups", "bond"), None, None),
            P(("groups", "bond"), None),
            P(("groups", "bond")),
        ),
        out_specs=(P(("groups", "bond"), None, None), P("groups")),
        check_vma=False,
    )
```

time: 776 us -> 139 us (0.18)
  waiting for transfers between devices: 541 us -> 0 us
  Pallas kernels: 0 us -> 129 us
  local copies, waits for them, and re-layouts: 89 us -> 1.2 us
  matrix products: 51.9 us -> 0 us
  blocking collectives: 35.8 us -> 0 us
  other arithmetic: 32.9 us -> 7.6 us
  between operations: 16.6 us -> 0.64 us
    all_to_all x1 -> x0, waiting for transfers between devices: 519 us -> none  [body(): lax.all_to_all(chosen, 'bond', split_axis=0, concat_axis=0, tiled=True)]
    pallas_call x0 -> x1, Pallas kernels: none -> 129 us  [fast_body(): pl.pallas_call(functools.partial(kernel, terms, sectors, phys), out_shape...]
    dot_general x2 -> x0, matrix products: 51.9 us -> none  [the longest x1 32.8 us: body(): jnp.einsum('ncaij,ncajk->ncik', outgoing, fetched, precision=lax.Precisio...]
    scatter x2 -> x0, local copies, waits for them, and re-layouts: 39.4 us -> none  [the longest x1 38.6 us: body(): outgoing = jnp.zeros((bond_count * capacity, term_count, states, states),...]
    psum x1 -> x0, blocking collectives: 22.2 us -> none  [body(): lax.psum((jnp.sum(psi_blocks * hpsi), jnp.sum(psi_blocks * psi_blocks)),...]
    psum x1 -> x0, waiting for transfers between devices: 22.2 us -> none  [body(): hpsi = lax.psum(partial_blocks, 'term')]
    select_n x3 -> x0, other arithmetic: 21.5 us -> none  [the longest x2 20.9 us: body(): jnp.take(right_env, lax.all_to_all(sector_ids, 'bond', split_axis=0, conc...]
    reshape x1 -> x0, local copies, waits for them, and re-layouts: 18.6 us -> none  [body(): products = products.reshape(block_count, term_count, states, states)]
  transfers between devices with their start and end apart: 2 -> 0, of which waited for: 2 -> 0; matrix products, arithmetic and copies ran while one was open for 12% -> 0% of each run, Pallas kernels for 0% -> 0%
where the time goes in v1:
time: 139 us
  Pallas kernels  129 us (93%)
  other arithmetic  7.6 us (5%)
    pallas_call x1, Pallas kernels, fast_body(): pl.pallas_call(functools.partial(kernel, terms, sectors, phys), out_shape...  129 us
    sub x1, other arithmetic, fast_body(): residual = part + other - value * psi_blocks  6.41 us

profile of v1, /device:TPU:0, one launch (start us, length us, event | category | flops | bytes accessed | tf_op | source)
XLA Modules:
  0.0 138.9 jit_solution(3187464302879663299)
XLA Ops:
  0.6 1.2 bitcast_add_fusion.idx_ref
  1.8 0.0 copy-start
  1.8 129.4 %shard_map.68 = (f32[48,128,128]{2,1,0:T(8,128)}, f32[48,128,128]{2,1,0:T(8,128)}, f32[8,128]{1,0:T(8,128)}) custom-call(s32[48]{0:T(128)} %bitcast_add_fusion.idx_ref, f32[48,128,128]{2,1,0:T(8,128)} %psi_hbm.1, f32[6,3,128,128]{3,2,1,0:T(8,128)} %left_hbm.1, f32[6,3,128,128]{3,2,1,0:T(8,128)} %right_hbm.1), custom_call_target="tpu_custom_call" | custom-call | flops 2415919104 | bytes 20000000 | tf_op jit(solution)/shard_map/pallas_call | solution.py:294
  131.3 1.2 slice.3
  132.4 0.0 copy-done
  132.4 6.4 %multiply_subtract_fusion = f32[48,128,128]{2,1,0:T(8,128)} fusion(f32[48,128,128]{2,1,0:T(8,128)S(1)} %copy-done, f32[48,128,128]{2,1,0:T(8,128)} %get-tuple-element.5, f32[48,128,128]{2,1,0:T(8,128)} %get-tuple-element.6, f32[]{:T(128)} %bitcast.1), kind=kLoop, calls=%fused_computation | loop fusion | flops 2359296 | bytes 12582916 | tf_op jit(solution)/shard_map/sub | solution.py:323
Async XLA Ops:
  1.8 130.6 %copy-start = (f32[48,128,128]{2,1,0:T(8,128)S(1)}, f32[48,128,128]{2,1,0:T(8,128)}, u32[]{:S(2)}) copy-start(f32[48,128,128]{2,1,0:T(8,128)} %psi_hbm.1) | copy-start | bytes 9437188

commit v2 on v1

--- a/solution.py
+++ b/solution.py
@@ -21,9 +21,13 @@
 
 
 def pair_rhs(x):
+    row = wide(x)
+    return jnp.concatenate([row, row], axis=0)
+
+
+def wide(x):
     hi, lo = split(x)
-    row = jnp.concatenate([hi, lo], axis=1)
-    return jnp.concatenate([row, row], axis=0)
+    return jnp.concatenate([hi, lo], axis=1)
 
 
 def fold(o):
@@ -36,10 +40,10 @@
     return jnp.sum(x.reshape(r // 8, 8, c), axis=0)
 
 
-def kernel(terms, sectors, phys, idx_ref, psi_hbm, left_hbm, right_hbm,
-           part_hbm, other_hbm, theta_ref, *scratch):
+def kernel(terms, sectors, phys, owner_ref, local_ref, psi_hbm, left_hbm, right_hbm,
+           out_hbm, theta_ref, *scratch):
     gathered = scratch[:terms]
-    (psi_v, left_v, lefts, prods, acc, dots,
+    (psi_v, left_v, lefts, prods, acc, other, dots,
      recv, send, psi_sem, left_sem, own_sem, xsend, xrecv, out_sem, dsend, drecv) = scratch[terms:]
     bond_count = NZ * NY
     blocks = sectors * phys
@@ -125,32 +129,45 @@
 
     def left_piece(s, lo, count):
         def body(i, norm):
-            b = s * phys + lo + i
-            x = psi_v[b]
-            t = fold(jnp.dot(lefts[s], pair_rhs(x), preferred_element_type=F32))
-            hi, low = split(t)
-            both = jnp.concatenate([hi, low], axis=1)
-            for a in range(terms):
-                prods[a, b] = both[a * states:(a + 1) * states]
-            return norm + rows_sum(x * x)
-
-        norm = lax.fori_loop(0, count, body, jnp.zeros((8, states), F32))
+            found = []
+            for u in range(2):
+                b = s * phys + lo + 2 * i + u
+                x = psi_v[b]
+                t = fold(jnp.dot(lefts[s], pair_rhs(x), preferred_element_type=F32))
+                found.append((b, split(t)))
+                norm = norm + rows_sum(x * x)
+            for b, (hi, low) in found:
+                for a in range(terms):
+                    cols = slice(a % 2 * states, (a % 2 + 1) * states)
+                    prods[a // 2, b, 0:states, cols] = hi[a * states:(a + 1) * states]
+                    prods[a // 2, b, states:2 * states, cols] = low[a * states:(a + 1) * states]
+            return norm
+
+        norm = lax.fori_loop(0, count // 2, body, jnp.zeros((8, states), F32))
         dots[me * 2 + core, 8:16, :] += norm
 
-    def right_piece(a, first, count):
+    def right_piece(p, first, count):
+        final = 2 * p + 1 == last
+
         def body(i, dot):
-            b = first + i
-            w = pair_rhs(gathered[a][idx_ref[b]])
-            v = fold(jnp.dot(prods[a, b], w, preferred_element_type=F32))
-            if a > 0:
-                v = v + acc[b]
-            acc[b] = v
-            if a == last:
-                dot = dot + rows_sum(v * psi_v[b])
+            found = []
+            for u in range(4):
+                b = first + 4 * i + u
+                r = owner_ref[b, 0] * sectors + local_ref[b]
+                w = jnp.concatenate([wide(gathered[2 * p][r]), wide(gathered[2 * p + 1][r])], axis=0)
+                o = fold(jnp.dot(prods[p, b], w, preferred_element_type=F32))
+                v = o[:states] + o[states:]
+                if p > 0:
+                    v = v + acc[b]
+                if final:
+                    dot = dot + rows_sum(v * psi_v[b])
+                found.append((b, v))
+            for b, v in found:
+                acc[b] = v
             return dot
 
-        dot = lax.fori_loop(0, count, body, jnp.zeros((8, states), F32))
-        if a == last:
+        dot = lax.fori_loop(0, count // 4, body, jnp.zeros((8, states), F32))
+        if final:
             dots[me * 2 + core, 0:8, :] += dot
 
     def across_done(a):
@@ -162,13 +179,11 @@
 
     def exchange_piece(k, first, count):
         c = pltpu.make_async_remote_copy(
-            src_ref=acc.at[pl.ds(first, count)], dst_ref=other_hbm.at[pl.ds(first, count)],
+            src_ref=acc.at[pl.ds(first, count)], dst_ref=other.at[pl.ds(first, count)],
             send_sem=xsend.at[k], recv_sem=xrecv.at[k],
             device_id={"term": 1 - core}, device_id_type=MESH)
         c.start()
-        d = pltpu.make_async_copy(acc.at[pl.ds(first, count)], part_hbm.at[pl.ds(first, count)], out_sem.at[k])
-        d.start()
-        exchange.append((c, d))
+        exchange.append(c)
 
     half = phys // 4
     left_work = []
@@ -180,23 +195,26 @@
                 left_piece(s, q * half, half)
             left_work.append(piece)
     eighth = blocks // 6
-
-    def right_work(a):
-        out = []
-        for q in range(6):
-            def piece(a=a, q=q):
-                if q == 0:
-                    across_done(a)
-                right_piece(a, q * eighth, eighth)
-            out.append(piece)
-        return out
+    twelve = blocks // 4
 
     slots = {(a, k): [] for a in range(terms) for k in range(6)}
     for i, w in enumerate(left_work):
         slots[(i // 6, i % 6)].append(w)
-    for a in range(terms - 2):
-        for i, w in enumerate(right_work(a)):
-            slots[(a + 2, i)].append(w)
+    for q in range(4):
+        def first_pair(q=q):
+            if q == 0:
+                across_done(0)
+                across_done(1)
+            right_piece(0, q * twelve, twelve)
+
+        def second_pair(q=q):
+            if q == 0:
+                across_done(2)
+                across_done(3)
+            right_piece(1, q * twelve, twelve)
+
+        slots[(3, q)].append(first_pair)
+        slots[(5, 2 + q)].append(second_pair)
 
     go(None, 0, me, ACROSS, True)
     go(z < NZ - 1, 0, me, UP, True)
@@ -238,11 +256,10 @@
             for w in slots[(a, 2 * h - 1)]:
                 w()
 
-    for w in right_work(last - 1):
-        w()
+    across_done(last - 1)
     own_copies[last].wait()
     for q in range(6):
-        right_piece(last, q * eighth, eighth)
+        right_piece(last // 2, q * eighth, eighth)
         exchange_piece(q, q * eighth, eighth)
 
     mine = me * 2 + core
@@ -265,7 +282,21 @@
         total = total + dots[i]
     dot = jnp.sum(total[0:8], axis=(0, 1), keepdims=True)
     norm = jnp.sum(total[8:16], axis=(0, 1), keepdims=True) * 0.5
-    theta_ref[...] = jnp.broadcast_to(dot / norm, theta_ref.shape)
+    theta = dot / norm
+    theta_ref[0] = theta[0, 0]
+    outs = []
+    for q in range(6):
+        exchange[q].wait()
+
+        def finish_block(i, carry, q=q):
+            b = q * eighth + i
+            acc[b] = acc[b] + other[b] - theta * psi_v[b]
+            return carry
+
+        lax.fori_loop(0, eighth, finish_block, 0)
+        d = pltpu.make_async_copy(acc.at[pl.ds(q * eighth, eighth)], out_hbm.at[pl.ds(q * eighth, eighth)], out_sem.at[q])
+        d.start()
+        outs.append(d)
 
     for cond, a, src, way, own in sent:
         def finish(a=a, src=src, way=way, own=own):
@@ -275,8 +306,7 @@
             finish()
         else:
             pl.when(cond)(finish)
-    for c, d in exchange:
-        c.wait()
+    for d in outs:
         d.wait()
     for c in dot_copies:
         c.wait_send()
@@ -287,20 +317,20 @@
     terms, sectors = left_env.shape[0], left_env.shape[1]
     phys = blocks // sectors
     bond_count = NZ * NY
-    right_sector = owner_route[:, 0] * sectors + local_sector
     any_spec = pl.BlockSpec(memory_space=pl.ANY)
     block_shape = jax.ShapeDtypeStruct((blocks, states, states), F32)
     dma = pltpu.SemaphoreType.DMA
-    part, other, theta = pl.pallas_call(
+    return pl.pallas_call(
         functools.partial(kernel, terms, sectors, phys),
-        out_shape=(block_shape, block_shape, jax.ShapeDtypeStruct((8, 128), F32)),
-        in_specs=[pl.BlockSpec(memory_space=pltpu.SMEM), any_spec, any_spec, any_spec],
-        out_specs=(any_spec, any_spec, pl.BlockSpec(memory_space=pltpu.VMEM)),
+        out_shape=(block_shape, jax.ShapeDtypeStruct((1,), F32)),
+        in_specs=[pl.BlockSpec(memory_space=pltpu.SMEM), pl.BlockSpec(memory_space=pltpu.SMEM), any_spec, any_spec, any_spec],
+        out_specs=(any_spec, pl.BlockSpec(memory_space=pltpu.SMEM)),
         scratch_shapes=[pltpu.VMEM((bond_count * sectors, states, states), F32) for _ in range(terms)] + [
             pltpu.VMEM((blocks, states, states), F32),
             pltpu.VMEM((terms, sectors, states, states), F32),
             pltpu.VMEM((sectors, terms * states, 2 * states), BF16),
-            pltpu.VMEM((terms, blocks, states, 2 * states), BF16),
+            pltpu.VMEM((terms // 2, blocks, 2 * states, 2 * states), BF16),
+            pltpu.VMEM((blocks, states, states), F32),
             pltpu.VMEM((blocks, states, states), F32),
             pltpu.VMEM((2 * bond_count, 16, states), F32),
             dma((terms, bond_count)),
@@ -318,10 +348,7 @@
             collective_id=0, has_side_effects=True, vmem_limit_bytes=56 * 1024 * 1024),
         cost_estimate=pl.CostEstimate(
             flops=4 * terms * blocks * states ** 3, bytes_accessed=20_000_000, transcendentals=0),
-    )(right_sector, psi_blocks, left_env, right_env)
-    value = theta[0, 0]
-    residual = part + other - value * psi_blocks
-    return residual, jnp.reshape(value, (1,))
+    )(owner_route, local_sector, psi_blocks, left_env, right_env)
 
 
 def general_body(psi_blocks, left_env, right_env, owner_route, local_sector):

time: 139 us -> 121 us (0.87)
  Pallas kernels: 129 us -> 113 us
  other arithmetic: 7.6 us -> 0 us
  local copies, waits for them, and re-layouts: 1.2 us -> 5.26 us
  between operations: 0.64 us -> 2.39 us
    pallas_call x1, Pallas kernels: 129 us -> 113 us  [fast_body(): pl.pallas_call(functools.partial(kernel, terms, sectors, phys), out_shape...]
    sub x1 -> x0, other arithmetic: 6.41 us -> none  [fast_body(): residual = part + other - value * psi_blocks]
    unnamed x2, local copies, waits for them, and re-layouts: 0.01 us -> 5.26 us
where the time goes in v2:
time: 121 us
  Pallas kernels  113 us (93%)
  local copies, waits for them, and re-layouts  5.26 us (4%)
  between operations  2.39 us (2%)
    pallas_call x1, Pallas kernels, fast_body(): pl.pallas_call(functools.partial(kernel, terms, sectors, phys), out_shape...  113 us
    unnamed x2, local copies, waits for them, and re-layouts  5.26 us

profile of v2, /device:TPU:0, one launch (start us, length us, event | category | flops | bytes accessed | tf_op | source)
XLA Modules:
  0.0 120.7 jit_solution(10437999205647721696)
XLA Ops:
  0.6 1.3 %copy.7.owner_ref = s32[48,1]{1,0:T(8,128)} copy(s32[48,1]{0,1:T(1,128)} %param.8) | data formatting | bytes 384 | tf_op args[3]
  2.0 113.0 %shard_map.68 = (f32[48,128,128]{2,1,0:T(8,128)}, f32[1]{0:T(128)}) custom-call(s32[48,1]{1,0:T(8,128)} %copy.7.owner_ref, s32[48]{0:T(128)} %local_ref.1, f32[48,128,128]{2,1,0:T(8,128)} %psi_hbm.1, f32[6,3,128,128]{3,2,1,0:T(8,128)} %left_hbm.1, f32[6,3,128,128]{3,2,1,0:T(8,128)} %right_hbm.1), custom_call_target="tpu_custom_call" | custom-call | flops 2415919104 | bytes 20000000 | tf_op jit(solution)/shard_map/pallas_call | solution.py:323
  115.0 3.9 %copy.10 = f32[48,128,128]{2,1,0:T(8,128)} copy(f32[48,128,128]{2,1,0:T(8,128)} %get-tuple-element.4) | data formatting | bytes 6291456

commit v3 on v2

--- a/solution.py
+++ b/solution.py
@@ -153,7 +153,7 @@
             found = []
             for u in range(4):
                 b = first + 4 * i + u
-                r = owner_ref[b, 0] * sectors + local_ref[b]
+                r = owner_ref[b] * sectors + local_ref[b]
                 w = jnp.concatenate([wide(gathered[2 * p][r]), wide(gathered[2 * p + 1][r])], axis=0)
                 o = fold(jnp.dot(prods[p, b], w, preferred_element_type=F32))
                 v = o[:states] + o[states:]
@@ -271,6 +271,19 @@
             device_id={"bond": pb, "term": pt}, device_id_type=MESH)
         c.start()
         dot_copies.append(c)
+    outs = []
+    for q in range(6):
+        exchange[q].wait()
+
+        def finish_block(i, carry, q=q):
+            b = q * eighth + i
+            acc[b] = acc[b] + other[b]
+            return carry
+
+        lax.fori_loop(0, eighth, finish_block, 0)
+        d = pltpu.make_async_copy(acc.at[pl.ds(q * eighth, eighth)], out_hbm.at[pl.ds(q * eighth, eighth)], out_sem.at[q])
+        d.start()
+        outs.append(d)
     for k, (pb, pt) in enumerate(peers):
         theirs = pb * 2 + pt
         pltpu.make_async_remote_copy(
@@ -284,20 +297,6 @@
     norm = jnp.sum(total[8:16], axis=(0, 1), keepdims=True) * 0.5
     theta = dot / norm
     theta_ref[0] = theta[0, 0]
-    outs = []
-    for q in range(6):
-        exchange[q].wait()
-
-        def finish_block(i, carry, q=q):
-            b = q * eighth + i
-            acc[b] = acc[b] + other[b] - theta * psi_v[b]
-            return carry
-
-        lax.fori_loop(0, eighth, finish_block, 0)
-        d = pltpu.make_async_copy(acc.at[pl.ds(q * eighth, eighth)], out_hbm.at[pl.ds(q * eighth, eighth)], out_sem.at[q])
-        d.start()
-        outs.append(d)
-
     for cond, a, src, way, own in sent:
         def finish(a=a, src=src, way=way, own=own):
             chunk(a, src, way, own).wait_send()
@@ -320,7 +319,7 @@
     any_spec = pl.BlockSpec(memory_space=pl.ANY)
     block_shape = jax.ShapeDtypeStruct((blocks, states, states), F32)
     dma = pltpu.SemaphoreType.DMA
-    return pl.pallas_call(
+    hpsi, theta = pl.pallas_call(
         functools.partial(kernel, terms, sectors, phys),
         out_shape=(block_shape, jax.ShapeDtypeStruct((1,), F32)),
         in_specs=[pl.BlockSpec(memory_space=pltpu.SMEM), pl.BlockSpec(memory_space=pltpu.SMEM), any_spec, any_spec, any_spec],
@@ -348,7 +347,8 @@
             collective_id=0, has_side_effects=True, vmem_limit_bytes=56 * 1024 * 1024),
         cost_estimate=pl.CostEstimate(
             flops=4 * terms * blocks * states ** 3, bytes_accessed=20_000_000, transcendentals=0),
-    )(owner_route, local_sector, psi_blocks, left_env, right_env)
+    )(owner_route.reshape(blocks), local_sector, psi_blocks, left_env, right_env)
+    return hpsi - theta[0] * psi_blocks, theta
 
 
 def general_body(psi_blocks, left_env, right_env, owner_route, local_sector):

time: 121 us -> 119 us (0.983)
  local copies, waits for them, and re-layouts: 5.26 us -> 0.01 us
  other arithmetic: 0 us -> 5.06 us
  Pallas kernels: 113 us -> 111 us
    unnamed x2, local copies, waits for them, and re-layouts: 5.26 us -> 0.01 us
    sub x0 -> x1, other arithmetic: none -> 5.06 us  [fast_body(): return (hpsi - theta[0] * psi_blocks, theta)]
    pallas_call x1, Pallas kernels: 113 us -> 111 us  [fast_body(): pl.pallas_call(functools.partial(kernel, terms, sectors, phys), out_shape...]
where the time goes in v3:
time: 119 us
  Pallas kernels  111 us (93%)
  other arithmetic  5.06 us (4%)
  between operations  2.47 us (2%)
    pallas_call x1, Pallas kernels, fast_body(): pl.pallas_call(functools.partial(kernel, terms, sectors, phys), out_shape...  111 us
    sub x1, other arithmetic, fast_body(): return (hpsi - theta[0] * psi_blocks, theta)  5.06 us

profile of v3, /device:TPU:0, one launch (start us, length us, event | category | flops | bytes accessed | tf_op | source)
XLA Modules:
  0.0 118.6 jit_solution(3543378362170425519)
XLA Ops:
  0.6 0.0 copy-start
  0.6 111.1 %shard_map.68 = (f32[48,128,128]{2,1,0:T(8,128)}, f32[1]{0:T(128)}) custom-call(s32[48]{0:T(128)} %bitcast.2, s32[48]{0:T(128)} %local_ref.1, f32[48,128,128]{2,1,0:T(8,128)} %psi_hbm.1, f32[6,3,128,128]{3,2,1,0:T(8,128)} %left_hbm.1, f32[6,3,128,128]{3,2,1,0:T(8,128)} %right_hbm.1), custom_call_target="tpu_custom_call" | custom-call | flops 2415919104 | bytes 20000000 | tf_op jit(solution)/shard_map/pallas_call | solution.py:322
  111.8 0.0 copy-done
  111.8 5.1 %multiply_subtract_fusion = f32[48,128,128]{2,1,0:T(8,128)} fusion(f32[48,128,128]{2,1,0:T(8,128)} %get-tuple-element.4, f32[48,128,128]{2,1,0:T(8,128)S(1)} %copy-done, f32[]{:T(128)} %bitcast.1), kind=kLoop, calls=%fused_computation | loop fusion | flops 1572864 | bytes 9437188 | tf_op jit(solution)/shard_map/sub | solution.py:351
Async XLA Ops:
  0.6 111.1 %copy-start = (f32[48,128,128]{2,1,0:T(8,128)S(1)}, f32[48,128,128]{2,1,0:T(8,128)}, u32[]{:S(2)}) copy-start(f32[48,128,128]{2,1,0:T(8,128)} %psi_hbm.1) | copy-start | bytes 9437188

commit v4 on v3

--- a/solution.py
+++ b/solution.py
@@ -151,8 +151,8 @@
 
         def body(i, dot):
             found = []
-            for u in range(4):
-                b = first + 4 * i + u
+            for u in range(8):
+                b = first + 8 * i + u
                 r = owner_ref[b] * sectors + local_ref[b]
                 w = jnp.concatenate([wide(gathered[2 * p][r]), wide(gathered[2 * p + 1][r])], axis=0)
                 o = fold(jnp.dot(prods[p, b], w, preferred_element_type=F32))
@@ -166,7 +166,7 @@
                 acc[b] = v
             return dot
 
-        dot = lax.fori_loop(0, count // 4, body, jnp.zeros((8, states), F32))
+        dot = lax.fori_loop(0, count // 8, body, jnp.zeros((8, states), F32))
         if final:
             dots[me * 2 + core, 0:8, :] += dot
 
@@ -195,26 +195,26 @@
                 left_piece(s, q * half, half)
             left_work.append(piece)
     eighth = blocks // 6
-    twelve = blocks // 4
+    third = blocks // 3
 
     slots = {(a, k): [] for a in range(terms) for k in range(6)}
     for i, w in enumerate(left_work):
         slots[(i // 6, i % 6)].append(w)
-    for q in range(4):
+    for q in range(3):
         def first_pair(q=q):
             if q == 0:
                 across_done(0)
                 across_done(1)
-            right_piece(0, q * twelve, twelve)
+            right_piece(0, q * third, third)
 
         def second_pair(q=q):
             if q == 0:
                 across_done(2)
                 across_done(3)
-            right_piece(1, q * twelve, twelve)
+            right_piece(1, q * third, third)
 
         slots[(3, q)].append(first_pair)
-        slots[(5, 2 + q)].append(second_pair)
+        slots[(5, 1 + q)].append(second_pair)
 
     go(None, 0, me, ACROSS, True)
     go(z < NZ - 1, 0, me, UP, True)

time: 119 us -> 116 us (0.975)
  Pallas kernels: 111 us -> 108 us
    pallas_call x1, Pallas kernels: 111 us -> 108 us  [fast_body(): pl.pallas_call(functools.partial(kernel, terms, sectors, phys), out_shape...]
where the time goes in v4:
time: 116 us
  Pallas kernels  108 us (93%)
  other arithmetic  5.06 us (4%)
  between operations  2.47 us (2%)
    pallas_call x1, Pallas kernels, fast_body(): pl.pallas_call(functools.partial(kernel, terms, sectors, phys), out_shape...  108 us
    sub x1, other arithmetic, fast_body(): return (hpsi - theta[0] * psi_blocks, theta)  5.06 us

profile of v4, /device:TPU:0, one launch (start us, length us, event | category | flops | bytes accessed | tf_op | source)
XLA Modules:
  0.0 115.8 jit_solution(3697062121357844614)
XLA Ops:
  0.6 0.0 copy-start
  0.6 108.3 %shard_map.68 = (f32[48,128,128]{2,1,0:T(8,128)}, f32[1]{0:T(128)}) custom-call(s32[48]{0:T(128)} %bitcast.2, s32[48]{0:T(128)} %local_ref.1, f32[48,128,128]{2,1,0:T(8,128)} %psi_hbm.1, f32[6,3,128,128]{3,2,1,0:T(8,128)} %left_hbm.1, f32[6,3,128,128]{3,2,1,0:T(8,128)} %right_hbm.1), custom_call_target="tpu_custom_call" | custom-call | flops 2415919104 | bytes 20000000 | tf_op jit(solution)/shard_map/pallas_call | solution.py:322
  108.9 0.0 copy-done
  108.9 5.1 %multiply_subtract_fusion = f32[48,128,128]{2,1,0:T(8,128)} fusion(f32[48,128,128]{2,1,0:T(8,128)} %get-tuple-element.4, f32[48,128,128]{2,1,0:T(8,128)S(1)} %copy-done, f32[]{:T(128)} %bitcast.1), kind=kLoop, calls=%fused_computation | loop fusion | flops 1572864 | bytes 9437188 | tf_op jit(solution)/shard_map/sub | solution.py:351
Async XLA Ops:
  0.6 108.3 %copy-start = (f32[48,128,128]{2,1,0:T(8,128)S(1)}, f32[48,128,128]{2,1,0:T(8,128)}, u32[]{:S(2)}) copy-start(f32[48,128,128]{2,1,0:T(8,128)} %psi_hbm.1) | copy-start | bytes 9437188
